TPU v7x, 32 devices: a whole 2x2x4 slice. The times are simulated.
32 devices in a mesh: parts: 2 (over y), lat: 2 (over core), lon: 8 (over z, x).
Axes of the slice: x: 2, y: 2, z: 4, core: 2. Of those that a mesh axis runs over, the one named last changes fastest.
Arguments:
- fields: bfloat16 [256, 64, 512], P(('parts', 'lat'), 'lon'), parts along dimension 0, may hold values from -6 to 6
- psi_near: bfloat16 [128, 4, 3, 3], replicated, may hold values from -2 to 2
- psi_far: bfloat16 [4, 2, 4, 3, 16], replicated, may hold values from -0.625 to 0.625
- blocks: int32 [4, 2], replicated, may hold values from 0 to 3, all different within a row
- weight: bfloat16 [4, 512, 512], replicated, may hold values from -0.125 to 0.125
- out_bias: float32 [512], replicated, may hold values from -6 to 6
- cotangent: bfloat16 [256, 64, 512], P(('parts', 'lat'), 'lon'), parts along dimension 0, may hold values from -6 to 6
Outputs:
- layer_out: bfloat16 [256, 64, 512], P(('parts', 'lat'), 'lon'), parts along dimension 0
- grad_fields: bfloat16 [256, 64, 512], P(('parts', 'lat'), 'lon'), parts along dimension 0
- grad_weight: float32 [4, 1024, 512], P(None, ('parts', 'lat', 'lon')), parts along dimension 1
- grad_bias: float32 [1024], P(('parts', 'lat', 'lon')), parts along dimension 0
There are 2 independent parts, one for each index of `parts`. A program takes and returns all parts, laid end to end along the dimension named above; an argument that names none is the same for every part. Nothing has to cross between parts.
Inputs may be any that keep to these rules, and one draw needn't show every extreme that they name: Each of the 4 polar rows names 2 different blocks; every block is named by some row.
All inputs are finite; a program needn't handle non-finite values.
Results may differ from a plain program's by a relative error of at most 0.005.
Values may be sent and summed in bfloat16 or wider, within the bound.
A program may use at most 128 MiB of HBM per device.

v0:
```python
import math

import jax
import jax.numpy as jnp
from jax import lax
from jax.sharding import PartitionSpec as P


def partner(shard, axis, bit):
    return lax.ppermute(shard, axis, [(i, i ^ 1 << bit) for i in range(lax.axis_size(axis))])


def with_halo(block, sides, width):
    for axis, dim in sides:
        count = lax.axis_size(axis)
        forward = [(i, i + 1) for i in range(count - 1)]
        forward.append((count - 1, 0))
        backward = [(target, source) for source, target in forward]
        low = lax.ppermute(
            lax.slice_in_dim(block, block.shape[dim] - width, None, axis=dim), axis, forward
        )
        high = lax.ppermute(lax.slice_in_dim(block, 0, width, axis=dim), axis, backward)
        block = jnp.concatenate([low, block, high], axis=dim)
    return block


def far_table(psi_far, blocks, circle_len):
    polar_count, block_count, basis_count, tap_count, block_width = psi_far.shape
    block_ids = jnp.arange(circle_len // block_width, dtype=jnp.int32)
    picker = (blocks[:, :, None] == block_ids[None, None, :]).astype(jnp.float32)
    dense_table = jnp.einsum("psb,pskwe->pkwbe", picker, psi_far.astype(jnp.float32))
    return dense_table.reshape(polar_count, basis_count, tap_count, circle_len).astype(jnp.bfloat16)


def far_coeffs(dense_table, out_lons, src_lons, circle_len):
    distance = (src_lons[None, :] - out_lons[:, None]) % circle_len
    return jnp.take(dense_table, distance, axis=3)


def far_forward(coeffs, polar_rows):
    zero_row = jnp.zeros((1,) + polar_rows.shape[1:], polar_rows.dtype)
    padded_rows = jnp.concatenate([zero_row, polar_rows], axis=0)
    polar_count = coeffs.shape[0]
    running = None
    for tap_row in range(3):
        tap_term = jnp.einsum(
            "pkjm,pmc->pjkc",
            coeffs[:, :, tap_row],
            padded_rows[tap_row : tap_row + polar_count],
            preferred_element_type=jnp.float32,
        )
        running = tap_term if running is None else running + tap_term
    return running


def far_adjoint(coeffs, polar_dz):
    running = None
    for tap_row in range(3):
        tap_term = jnp.einsum(
            "pkjm,pjkc->pmc", coeffs[:, :, tap_row], polar_dz, preferred_element_type=jnp.float32
        )
        tap_term = jnp.pad(tap_term, ((tap_row, 2 - tap_row), (0, 0), (0, 0)))
        running = tap_term if running is None else running + tap_term
    return running[1:]


def pick_edge(joined, at_pole):
    return jnp.where(at_pole, joined[joined.shape[0] - 1], joined[0])


def frame_rows(joined, edge_got, at_pole):
    zero_rim = jnp.zeros_like(edge_got)
    upper_rim = jnp.where(at_pole, zero_rim, edge_got)
    lower_rim = jnp.where(at_pole, edge_got, zero_rim)
    return jnp.concatenate([upper_rim[None], joined, lower_rim[None]], axis=0)


def on_device(fields, psi_near, psi_far, blocks, weight, out_bias, cotangent):
    row_count, lon_count, chan_count = fields.shape
    basis_count = weight.shape[0]
    polar_count = psi_far.shape[0]
    lon_devices = lax.axis_size("lon")
    lat_devices = lax.axis_size("lat")
    circle_len = lon_count * lon_devices
    lat_place = lax.axis_index("lat")
    lon_place = lax.axis_index("lon")
    at_pole = lat_place == 0
    cot_dz = jnp.einsum(
        "ijd,kcd->ijkc", cotangent, weight, preferred_element_type=jnp.float32
    ).astype(jnp.bfloat16)
    joined = jnp.concatenate(
        [fields, cot_dz.reshape(row_count, lon_count, basis_count * chan_count)], axis=2
    )
    edge_got = partner(pick_edge(joined, at_pole), "lat", 0)
    extended = frame_rows(joined, edge_got, at_pole)
    extended = with_halo(extended, (("lon", 1),), 1)
    field_ext = extended[:, :, :chan_count]
    dz_ext = extended[:, :, chan_count:].reshape(
        row_count + 2, lon_count + 2, basis_count, chan_count
    )
    psi_pad = jnp.pad(psi_near, ((1, 1), (0, 0), (0, 0), (0, 0)))
    psi_local = lax.dynamic_slice_in_dim(psi_pad, lat_place * row_count, row_count + 2, 0)
    tap_ids = jnp.arange(3, dtype=jnp.int32)
    out_ids = jnp.arange(lon_count, dtype=jnp.int32)
    ext_ids = jnp.arange(lon_count + 2, dtype=jnp.int32)
    forward_pick = (
        ext_ids[None, None, :] - out_ids[None, :, None] == tap_ids[:, None, None]
    ).astype(jnp.bfloat16)
    backward_pick = (
        out_ids[None, :, None] + 2 - ext_ids[None, None, :] == tap_ids[:, None, None]
    ).astype(jnp.bfloat16)
    near_band = jnp.einsum(
        "ikwe,ejn->ikwjn",
        psi_local[1 : row_count + 1],
        forward_pick,
        preferred_element_type=jnp.float32,
    ).astype(jnp.bfloat16)
    z_near = None
    dx_near = None
    for tap_row in range(3):
        tap_term = jnp.einsum(
            "ikjn,inc->ijkc",
            near_band[:, :, tap_row],
            field_ext[tap_row : tap_row + row_count],
            preferred_element_type=jnp.float32,
        )
        z_near = tap_term if z_near is None else z_near + tap_term
        psi_part = psi_local[2 - tap_row : 2 - tap_row + row_count, :, tap_row]
        back_band = jnp.einsum(
            "ake,ebn->akbn", psi_part, backward_pick, preferred_element_type=jnp.float32
        ).astype(jnp.bfloat16)
        back_term = jnp.einsum(
            "akbn,ankc->abc",
            back_band,
            dz_ext[2 - tap_row : 2 - tap_row + row_count],
            preferred_element_type=jnp.float32,
        )
        dx_near = back_term if dx_near is None else dx_near + back_term
    dense_table = far_table(psi_far, blocks, circle_len)
    polar_fields = fields[: polar_count + 1]
    polar_dz = cot_dz[:polar_count]
    own_lons = lon_place * lon_count + out_ids
    shard_piece = lax.all_gather(polar_fields, "lon", axis=1, tiled=True)
    src_lons = jnp.arange(shard_piece.shape[1], dtype=jnp.int32)
    coeffs = far_coeffs(dense_table, own_lons, src_lons, circle_len)
    far_z = far_forward(coeffs, shard_piece)
    src_lons = jnp.arange(lon_count * lax.axis_size("lon"), dtype=jnp.int32)
    coeffs = far_coeffs(dense_table, own_lons, src_lons, circle_len)
    far_dx = lax.psum_scatter(
        jnp.transpose(far_adjoint(coeffs, polar_dz), (1, 0, 2)),
        "lon",
        scatter_dimension=0,
        tiled=True,
    )
    far_dx = jnp.transpose(far_dx, (1, 0, 2))
    pole_mask = at_pole.astype(jnp.float32)
    far_z = far_z * pole_mask
    far_dx = far_dx * pole_mask
    z_full = z_near + jnp.pad(far_z, ((0, row_count - polar_count), (0, 0), (0, 0), (0, 0)))
    z_mix = z_full.astype(jnp.bfloat16)
    layer_out = (
        jnp.einsum("ijkc,kcd->ijd", z_mix, weight, preferred_element_type=jnp.float32) + out_bias
    ).astype(jnp.bfloat16)
    grad_fields = (
        dx_near + jnp.pad(far_dx, ((0, row_count - polar_count - 1), (0, 0), (0, 0)))
    ).astype(jnp.bfloat16)
    grad_scale = 1.0 / math.sqrt(row_count * lat_devices * circle_len)
    weight_term = (
        jnp.einsum("ijkc,ijd->kcd", z_mix, cotangent, preferred_element_type=jnp.float32)
        * grad_scale
    )
    bias_term = jnp.sum(cotangent, axis=(0, 1), dtype=jnp.float32) * grad_scale
    grad_weight, grad_bias = (
        lax.psum_scatter(weight_term, ("lat", "lon"), scatter_dimension=1, tiled=True),
        lax.psum_scatter(bias_term, ("lat", "lon"), scatter_dimension=0, tiled=True),
    )
    return (layer_out, grad_fields, grad_weight, grad_bias)


def solution(mesh):
    return jax.shard_map(
        on_device,
        mesh=mesh,
        in_specs=(
            P(("parts", "lat"), "lon", None),
            P(),
            P(),
            P(),
            P(),
            P(),
            P(("parts", "lat"), "lon", None),
        ),
        out_specs=(
            P(("parts", "lat"), "lon", None),
            P(("parts", "lat"), "lon", None),
            P(None, ("parts", "lat", "lon"), None),
            P(("parts", "lat", "lon")),
        ),
        check_vma=False,
    )
```

profile of v0, /device:TPU:0, one launch (start us, length us, event | category | flops | bytes accessed | tf_op | source)
XLA Modules:
  0.0 185.8 jit_solution(13403977840595174009)
XLA Ops:
  7.2 0.0 reduce-scatter.3.cloned.1.call-start
  7.2 1.5 copy-done
  8.8 2.3 %fusion.11 = bf16[64,8,4,512]{3,1,2,0:T(8,128)(2,1)S(1)} fusion(bf16[4,512,512]{2,1,0:T(8,128)(2,1)S(1)} %copy-done, bf16[64,8,512]{2,1,0:T(8,128)(2,1)} %param.15), kind=kOutput, calls=%fused_computation.15 | convolution fusion | flops 1074790400 | bytes 4718592 | tf_op jit(solution)/shard_map/ijd,kcd->ijkc/dot_general | solution.py:88
  11.1 1.3 copy-done.2
  12.5 0.5 collective-permute-start
  13.0 0.1 compare_and_fusion
  13.1 0.1 compare_select_fusion
  13.2 0.1 copy.48
  13.3 0.1 reshape.84
  13.4 0.3 fusion.47
  13.7 0.4 copy.91
  14.0 3.7 %gather_fusion = bf16[512,4,4,3]{2,1,3,0:T(4,128)(2,1)} fusion(bf16[4,4,3,64]{1,0,3,2:T(4,128)(2,1)S(1)} %bitcast.187, s32[1024]{0:T(1024)S(1)} %pad_clamp_fusion), kind=kCustom, calls=%fused_computation.clone | custom fusion | bytes 100352 | tf_op jit(solution)/shard_map/jit(_take)/gather | solution.py:37
  17.7 2.9 %copy.84 = bf16[8,64,4,4,3]{1,0,3,2,4:T(8,128)(2,1)S(1)} copy(bf16[8,64,4,4,3]{3,2,4,1,0:T(4,128)(2,1)} %bitcast.186) | data formatting | bytes 98304 | tf_op jit(solution)/shard_map/jit(_take)/gather | solution.py:37
  20.7 1.2 convolution_bitcast_fusion.1
  21.9 1.2 convolution_bitcast_fusion
  23.1 1.2 convolution_bitcast_fusion.2
  24.2 1.1 fusion.50
  25.3 0.0 reduce-scatter.5.cloned.1.call-start
  25.4 32.8 %all_gather.3 = bf16[5,64,512]{2,1,0:T(8,128)(2,1)S(1)} all-gather(bf16[5,8,512]{2,1,0:T(8,128)(2,1)S(1)} %slice-done), channel_id=1, replica_groups=mesh['parts'=2,'lat'=2,'lon'=8] {'lon'}, dimensions={1}, use_global_device_ids=true | all-gather | bytes 368640 | tf_op jit(solution)/shard_map/all_gather | solution.py:143
  58.2 0.1 convolution_bitcast_fusion.5
  58.4 0.9 fusion.46
  59.3 0.3 convolution_convert_fusion
  59.6 4.4 %pad_maximum_fusion.4 = (bf16[66,1,2560]{2,1,0:T(2,128)(2,1)S(1)}, bf16[66,1,2560]{2,1,0:T(2,128)(2,1)S(1)}) fusion(bf16[1,8,2560]{2,1,0:T(8,128)(2,1)S(1)} %get-tuple-element.14, bf16[1,8,2560]{2,1,0:T(8,128)(2,1)S(1)} %get-tuple-element.13, bf16[64,8,2048]{2,1,0:T(8,128)(2,1)} %bitcast.184, bf16[64,8,512]{2,1,0:T(8,128)(2,1)S(1)} %copy-done.5), kind=kLoop, calls=%fused_computation.50 | loop fusion | flops 2703360 | bytes 3379200 | tf_op jit(solution)/shard_map/slice | solution.py:20
  64.1 0.8 copy.40
  64.9 0.8 copy.41
  65.7 4.1 %collective-permute-start.2 = (bf16[66,1,2560]{2,0,1:T(8,128)(2,1)}, bf16[66,1,2560]{2,0,1:T(8,128)(2,1)}, u32[]{:S(2)}, u32[]{:S(2)}) collective-permute-start(bf16[66,1,2560]{2,0,1:T(8,128)(2,1)} %copy.41), channel_id=1, source_target_pairs={{1,0},{2,1},{3,2},{4,3},{5,4},{6,5},{7,6},{0,7},{9,8},{10,9},{11,1... | collective-permute-start | bytes 1013768 | tf_op jit(solution)/shard_map/ppermute | solution.py:22
  69.8 0.7 slice_bitcast_fusion.10
  70.5 1.8 copy.47
  72.4 2.5 %copy.46 = bf16[64,4,8,10]{3,2,1,0:T(8,128)(2,1)} copy(bf16[64,4,8,10]{0,3,2,1:T(8,128)(2,1)} %get-tuple-element.11) | data formatting | bytes 81920 | tf_op jit(solution)/shard_map/squeeze | solution.py:123
  74.9 2.5 %copy.45 = bf16[64,4,8,10]{3,2,1,0:T(8,128)(2,1)} copy(bf16[64,4,8,10]{0,3,2,1:T(8,128)(2,1)} %get-tuple-element.12) | data formatting | bytes 81920 | tf_op jit(solution)/shard_map/squeeze | solution.py:123
  77.5 1.3 fusion.45
  78.7 2.5 %collective-permute-done.2 = bf16[66,1,2560]{2,0,1:T(8,128)(2,1)} collective-permute-done((bf16[66,1,2560]{2,0,1:T(8,128)(2,1)}, bf16[66,1,2560]{2,0,1:T(8,128)(2,1)}, u32[]{:S(2)}, u32[]{:S(2)}) %collective-permute-start.2) | collective-permute-done | bytes 337952 | tf_op jit(solution)/shard_map/ppermute | solution.py:22
  81.2 1.5 copy.43
  82.7 1.5 copy.42
  84.3 5.1 %pad_maximum_fusion = bf16[66,10,2560]{2,1,0:T(8,128)(2,1)S(1)} fusion(bf16[66,1,2560]{2,1,0:T(2,128)(2,1)S(1)} %copy.43, bf16[1,8,2560]{2,1,0:T(8,128)(2,1)S(1)} %get-tuple-element.14, bf16[64,8,2048]{2,1,0:T(8,128)(2,1)S(1)} %bitcast.185, bf16[64,8,512]{2,1,0:T(8,128)(2,1)S(1)} %copy-done.5, bf16[1,8,2560]{2,1,0:T(8,128)(2,1)S(1)} %get-tuple-element.13, ...), kind=kLoop, calls=%fused_computation.1 | loop fusion | flops 20275200 | bytes 6758400 | tf_op jit(solution)/shard_map/concatenate | solution.py:23
  89.4 0.7 fusion.48
  90.1 0.7 copy-done.10
  90.8 0.7 fusion.49
  91.5 0.3 copy-done.1
  91.8 0.7 fusion.6
  92.5 1.3 copy-done.6
  93.8 3.4 %bitcast_multiply_fusion = f32[4,512,512]{2,1,0:T(8,128)} fusion(bf16[64,8,4,512]{3,1,2,0:T(8,128)(2,1)S(1)} %fusion.6, bf16[64,8,512]{2,1,0:T(8,128)(2,1)S(1)} %copy-done.12), kind=kOutput, calls=%fused_computation.2 | convolution fusion | flops 1074790400 | bytes 6815744 | tf_op jit(solution)/shard_map/ijkc,ijd->kcd/dot_general | solution.py:169
  97.2 0.6 copy-done.20
  97.8 0.6 dynamic-slice
  99.1 0.1 iota_subtract_fusion
  99.1 0.3 convolution_convert_fusion.2
  99.4 0.9 copy.57
  100.3 0.3 convolution_convert_fusion.3
  100.6 1.7 copy.54
  102.3 0.3 convolution_convert_fusion.1
  102.5 1.7 copy.60
  104.2 0.1 convert_reduce_fusion
  104.3 29.9 %all-reduce.7 = f32[512]{0:T(512)S(1)} all-reduce(f32[512]{0:T(512)S(1)} %broadcast_multiply_fusion), channel_id=4, replica_groups=mesh['parts'=2,'lat'=2,'lon'=8] {'lat','lon'}, use_global_device_ids=true, to_apply=%region_3.5.clone | all-reduce | flops 512 | bytes 4096
  134.3 0.6 dynamic-slice.1
  134.9 9.1 %fusion.90 = (bf16[64,10,2048]{2,1,0:T(8,128)(2,1)}, bf16[64,10,2048]{2,1,0:T(8,128)(2,1)}, bf16[64,10,2048]{2,1,0:T(8,128)(2,1)}) fusion(bf16[66,10,2560]{2,1,0:T(8,128)(2,1)} %copy-done.1), kind=kLoop, calls=%fused_computation.118 | loop fusion | bytes 15728640 | tf_op jit(solution)/shard_map/slice | solution.py:135
  143.9 7.7 %reshape.114 = bf16[64,10,4,512]{3,2,1,0:T(4,128)(2,1)} reshape(bf16[64,10,2048]{2,1,0:T(8,128)(2,1)} %get-tuple-element.5) | data formatting | bytes 5242880 | tf_op jit(solution)/shard_map/slice | solution.py:135
  151.6 7.7 %reshape.113 = bf16[64,10,4,512]{3,2,1,0:T(4,128)(2,1)} reshape(bf16[64,10,2048]{2,1,0:T(8,128)(2,1)} %get-tuple-element.6) | data formatting | bytes 5242880 | tf_op jit(solution)/shard_map/slice | solution.py:135
  159.3 7.7 %reshape.112 = bf16[64,10,4,512]{3,2,1,0:T(4,128)(2,1)} reshape(bf16[64,10,2048]{2,1,0:T(8,128)(2,1)} %get-tuple-element.7) | data formatting | bytes 5242880 | tf_op jit(solution)/shard_map/slice | solution.py:135
  167.0 3.3 %fusion.20 = f32[64,8,512]{2,1,0:T(8,128)S(1)} fusion(bf16[64,4,8,10]{3,2,1,0:T(8,128)(2,1)S(1)} %copy.57, bf16[64,10,4,512]{3,2,1,0:T(4,128)(2,1)} %reshape.113), kind=kOutput, calls=%fused_computation.18 | convolution fusion | flops 20971520 | bytes 3710976 | tf_op jit(solution)/shard_map/akbn,ankc->abc/dot_general | solution.py:132
  170.3 1.4 fusion.32
  171.7 0.2 copy-done.7
  172.0 2.0 %fusion.41 = bf16[64,8,512]{2,1,0:T(8,128)(2,1)} fusion(bf16[64,8,4,512]{3,1,2,0:T(8,128)(2,1)S(1)} %copy-done.7, bf16[4,512,512]{2,1,0:T(8,128)(2,1)S(1)} %copy-done, f32[512]{0:T(512)S(1)} %copy-done.19), kind=kOutput, calls=%fused_computation.25 | convolution fusion | flops 1074266112 | bytes 4720640 | tf_op jit(solution)/shard_map/ijkc,kcd->ijd/dot_general | solution.py:162
  174.0 0.9 multiply_bitcast_fusion
  174.9 4.1 %fusion.38 = bf16[64,8,512]{2,1,0:T(8,128)(2,1)} fusion(f32[64,8,512]{2,1,0:T(8,128)S(1)} %fusion.32, bf16[64,4,8,10]{3,2,1,0:T(8,128)(2,1)} %copy.60, bf16[64,10,4,512]{3,2,1,0:T(4,128)(2,1)} %reshape.114, f32[5,8,512]{2,1,0:T(8,128)S(1)} %multiply_bitcast_fusion), kind=kOutput, calls=%fused_computation.24 | convolution fusion | flops 21757952 | bytes 4317184 | tf_op jit(solution)/shard_map/akbn,ankc->abc/dot_general | solution.py:132
  (53 shorter events, 0.2 us)
Async XLA Ops:
  7.2 1.6 copy-start
  7.2 5.3 %copy-start.5 = (bf16[64,8,512]{2,1,0:T(8,128)(2,1)S(1)}, bf16[64,8,512]{2,1,0:T(8,128)(2,1)}, u32[]{:S(2)}) copy-start(bf16[64,8,512]{2,1,0:T(8,128)(2,1)} %param.9) | copy-start | bytes 1572868
  7.2 166.8 %reduce-scatter.3.cloned.1.call-start = ((), (), s32[]{:S(2)}) async-start(), calls=%async_computation.2 | async-start | bytes 737280 | tf_op jit(solution)/shard_map/reduce_scatter | solution.py:149
  8.8 4.4 %copy-start.17 = (s32[4,2]{0,1:T(2,128)S(1)}, s32[4,2]{0,1:T(2,128)}, u32[]{:S(2)}) copy-start(s32[4,2]{0,1:T(2,128)} %param.12) | copy-start | bytes 100
  8.8 4.6 %copy-start.18 = (bf16[4,2,4,3,16]{4,2,3,1,0:T(4,128)(2,1)S(1)}, bf16[4,2,4,3,16]{4,2,3,1,0:T(4,128)(2,1)}, u32[]{:S(2)}) copy-start(bf16[4,2,4,3,16]{4,2,3,1,0:T(4,128)(2,1)} %param.11) | copy-start | bytes 9220
  11.1 1.3 copy-start.2
  12.5 12.9 %copy-start.16 = (bf16[128,4,3,3]{0,1,3,2:T(4,128)(2,1)S(1)}, bf16[128,4,3,3]{0,1,3,2:T(4,128)(2,1)}, u32[]{:S(2)}) copy-start(bf16[128,4,3,3]{0,1,3,2:T(4,128)(2,1)} %param.10) | copy-start | bytes 27652
  12.5 12.9 %slice-start = ((bf16[64,8,512]{2,1,0:T(8,128)(2,1)}), bf16[5,8,512]{2,1,0:T(8,128)(2,1)S(1)}, s32[]{:S(2)}) async-start(bf16[64,8,512]{2,1,0:T(8,128)(2,1)} %param.9), calls=%async_computation.4 | async-start | bytes 81920 | tf_op jit(solution)/shard_map/slice | solution.py:140
  12.5 47.1 %collective-permute-start = (bf16[8,2560]{1,0:T(8,128)(2,1)S(1)}, bf16[8,2560]{1,0:T(8,128)(2,1)S(1)}, u32[]{:S(2)}, u32[]{:S(2)}) collective-permute-start(bf16[8,2560]{1,0:T(8,128)(2,1)S(1)} %fusion.59), channel_id=1, source_target_pairs={{0,8},{8,0},{1,9},{9,1},{2,10},{10,2},{3,11},{11,3},{4,12},{12,4},... | collective-permute-start | bytes 122888 | tf_op jit(solution)/shard_map/ppermute | solution.py:10
  20.7 43.4 %copy-start.11 = (bf16[4,4,3,8,64]{4,3,1,0,2:T(8,128)(2,1)}, bf16[4,4,3,8,64]{4,3,1,0,2:T(8,128)(2,1)S(1)}, u32[]{:S(2)}) copy-start(bf16[4,4,3,8,64]{4,3,1,0,2:T(8,128)(2,1)S(1)} %select_bitcast_fusion) | copy-start | bytes 147460
  25.3 153.7 %reduce-scatter.5.cloned.1.call-start = ((), (), s32[]{:S(2)}) async-start(), calls=%async_computation.3 | async-start | bytes 4456448 | tf_op jit(solution)/shard_map/reduce_scatter | solution.py:174
  25.4 40.2 %copy-start.14 = (bf16[128,4,3,3]{0,3,2,1:T(4,128)(2,1)}, bf16[128,4,3,3]{0,3,2,1:T(4,128)(2,1)S(1)}, u32[]{:S(2)}) copy-start(bf16[128,4,3,3]{0,3,2,1:T(4,128)(2,1)S(1)} %copy.44) | copy-start | bytes 27652
  65.7 15.5 %collective-permute-start.2 = (bf16[66,1,2560]{2,0,1:T(8,128)(2,1)}, bf16[66,1,2560]{2,0,1:T(8,128)(2,1)}, u32[]{:S(2)}, u32[]{:S(2)}) collective-permute-start(bf16[66,1,2560]{2,0,1:T(8,128)(2,1)} %copy.41), channel_id=1, source_target_pairs={{1,0},{2,1},{3,2},{4,3},{5,4},{6,5},{7,6},{0,7},{9,8},{10,9},{11,1... | collective-permute-start | bytes 1013768 | tf_op jit(solution)/shard_map/ppermute | solution.py:22
  69.8 12.9 %collective-permute-start.1 = (bf16[66,1,2560]{2,0,1:T(8,128)(2,1)}, bf16[66,1,2560]{2,0,1:T(8,128)(2,1)}, u32[]{:S(2)}, u32[]{:S(2)}) collective-permute-start(bf16[66,1,2560]{2,0,1:T(8,128)(2,1)} %copy.40), channel_id=1, source_target_pairs={{0,1},{1,2},{2,3},{3,4},{4,5},{5,6},{6,7},{7,0},{8,9},{9,10},{10,1... | collective-permute-start | bytes 1013768 | tf_op jit(solution)/shard_map/ppermute | solution.py:19
  77.5 6.8 %copy-start.3 = (bf16[64,8,4,512]{3,1,2,0:T(8,128)(2,1)S(1)}, bf16[64,8,4,512]{3,1,2,0:T(8,128)(2,1)}, u32[]{:S(2)}) copy-start(bf16[64,8,4,512]{3,1,2,0:T(8,128)(2,1)} %copy-done.2) | copy-start | bytes 6291460
  84.3 5.1 %copy-start.9 = (bf16[64,4,8,10]{3,2,1,0:T(8,128)(2,1)S(1)}, bf16[64,4,8,10]{3,2,1,0:T(8,128)(2,1)}, u32[]{:S(2)}) copy-start(bf16[64,4,8,10]{3,2,1,0:T(8,128)(2,1)} %copy.46) | copy-start | bytes 122884
  89.4 2.4 %copy-start.1 = (bf16[66,10,2560]{2,1,0:T(8,128)(2,1)}, bf16[66,10,2560]{2,1,0:T(8,128)(2,1)S(1)}, u32[]{:S(2)}) copy-start(bf16[66,10,2560]{2,1,0:T(8,128)(2,1)S(1)} %pad_maximum_fusion) | copy-start | bytes 10137604
  89.4 1.4 copy-start.10
  91.8 2.1 %copy-start.12 = (bf16[64,8,512]{2,1,0:T(8,128)(2,1)S(1)}, bf16[64,8,512]{2,1,0:T(8,128)(2,1)}, u32[]{:S(2)}) copy-start(bf16[64,8,512]{2,1,0:T(8,128)(2,1)} %param.15) | copy-start | bytes 1572868
  92.5 1.3 copy-start.6
  97.2 0.7 copy-start.20
  97.2 2.0 %copy-start.15 = (bf16[128,4,3,3]{0,3,2,1:T(4,128)(2,1)S(1)}, bf16[128,4,3,3]{0,3,2,1:T(4,128)(2,1)}, u32[]{:S(2)}) copy-start(bf16[128,4,3,3]{0,3,2,1:T(4,128)(2,1)} %copy-done.14) | copy-start | bytes 27652
  97.2 7.0 %copy-start.13 = (bf16[64,8,512]{2,1,0:T(8,128)(2,1)S(1)}, bf16[64,8,512]{2,1,0:T(8,128)(2,1)}, u32[]{:S(2)}) copy-start(bf16[64,8,512]{2,1,0:T(8,128)(2,1)} %param.15) | copy-start | bytes 1572868
  167.0 3.3 %copy-start.4 = (bf16[64,10,4,512]{3,2,1,0:T(4,128)(2,1)S(1)}, bf16[64,10,4,512]{3,2,1,0:T(4,128)(2,1)}, u32[]{:S(2)}) copy-start(bf16[64,10,4,512]{3,2,1,0:T(4,128)(2,1)} %reshape.112) | copy-start | bytes 7864324
  167.0 3.3 %copy-start.8 = (bf16[64,4,8,10]{3,2,1,0:T(8,128)(2,1)S(1)}, bf16[64,4,8,10]{3,2,1,0:T(8,128)(2,1)}, u32[]{:S(2)}) copy-start(bf16[64,4,8,10]{3,2,1,0:T(8,128)(2,1)} %copy.54) | copy-start | bytes 122884
  170.3 1.6 copy-start.7
  170.3 1.6 copy-start.19
Sparse Core Ops, SparseCore 0:
  25.4 69.2 reduce-scatter.2
  99.7 71.6 reduce-scatter.4
where the time goes:
time: 189 us; the launch traced here: 186 us
  local copies, waits for them, and re-layouts  63.1 us (33%)
  blocking collectives  62.7 us (33%)
  matrix products  25.8 us (14%)
  between operations  15.1 us (8%)
  other arithmetic  11.9 us (6%)
  starting transfers between devices  4.72 us (2%)
  waiting for transfers between devices  2.5 us (1%)
    all_gather x1, blocking collectives, on_device(): shard_piece = lax.all_gather(polar_fields, 'lon', axis=1, tiled=True)  32.8 us
    slice x4, local copies, waits for them, and re-layouts, on_device(): dz_ext[2 - tap_row:2 - tap_row + row_count]  32.2 us
    unnamed x1, blocking collectives  29.9 us
    dot_general x3, matrix products, on_device(): jnp.einsum('akbn,ankc->abc', back_band, dz_ext[2 - tap_row:2 - tap_row +...  8.76 us
    squeeze x4, local copies, waits for them, and re-layouts, on_device(): near_band[:, :, tap_row]  7.65 us
    unnamed x46, local copies, waits for them, and re-layouts  7.36 us
    gather x2, local copies, waits for them, and re-layouts, far_coeffs(): return jnp.take(dense_table, distance, axis=3)  6.59 us
    concatenate x1, other arithmetic, with_halo(): block = jnp.concatenate([low, block, high], axis=dim)  5.08 us
  transfers between devices with their start and end apart: 5, of which 1 were waited for; matrix products, arithmetic and copies ran while one was open for 50% of the time, Pallas kernels for 0%

commit v1 on v0

v1 whole, which is shorter than its diff:
```python
import functools
import math

import jax
import jax.numpy as jnp
from jax import lax
from jax.experimental import pallas as pl
from jax.experimental.pallas import tpu as pltpu
from jax.sharding import PartitionSpec as P

F32 = jnp.float32
BF16 = jnp.bfloat16
MESH = pl.DeviceIdType.MESH
BR = 8
FROWS = 6
CROWS = 4
GROUP = 8


def dot(a, b):
    return jnp.dot(a, b, preferred_element_type=F32)


def kernel(
    n, nrow, nl, kk, scale,
    x_ref, g_ref, e_ref, p_ref, t_ref, w_ref, b_ref,
    out_ref, gf_ref, gw_ref, gb_ref,
    hal, polf, polc, a_own, a_lr, a_t, a_j, a_farf, a_farc, zs, edge_acc,
    s0, r0, own, s1, r1, s2, r2, bsend, brecv,
    h_send, h_recv, p_send, p_recv, send0, recv0, send1, recv1, send2, recv2, b_ssem, b_rsem,
):
    part = lax.axis_index("parts")
    lat = lax.axis_index("lat")
    lon = lax.axis_index("lon")
    other = 1 - lat
    chan = x_ref.shape[1]
    half = chan // 2
    circle = n * nl
    nb = nrow // BR
    m = BR * nl * kk
    cells = BR * nl
    right = lax.rem(lon + 1, n)
    left = lax.rem(lon + n - 1, n)
    mine = lat * n + lon
    par = lax.rem(lon, 2)
    zz = lon // 2
    nz = n // 2
    rcp = pltpu.make_async_remote_copy

    barrier = pltpu.get_barrier_semaphore()

    def greet(step, _):
        to = lax.rem(mine + step, 2 * n)
        pl.semaphore_signal(
            barrier, inc=1, device_id=(part, to // n, lax.rem(to, n)), device_id_type=MESH
        )
        return 0

    lax.fori_loop(1, 2 * n, greet, 0)
    bsend[...] = jnp.broadcast_to(
        jnp.sum(g_ref[...].astype(F32), axis=0, keepdims=True), bsend.shape
    )
    pl.semaphore_wait(barrier, 2 * n - 1)

    srcs = (x_ref, g_ref)
    cut = pl.multiple_of(other * (nrow - 16), 16)
    cell_cut = pl.multiple_of(other * (nrow * nl - 16), 16)
    halo = []
    for d in range(2):
        first = e_ref.at[2 * d]
        last = e_ref.at[2 * d + 1]
        moves = (
            (last, 0, nrow, (part, lat, right)),
            (first, nrow, nrow, (part, lat, left)),
            (last.at[pl.ds(cut, 16)], 2 * nrow, 16, (part, other, right)),
            (first.at[pl.ds(cut, 16)], 2 * nrow + 16, 16, (part, other, left)),
            (srcs[d].at[pl.ds(cell_cut, 16)], 2 * nrow + 32, 16, (part, other, lon)),
        )
        for s, (src, start, size, to) in enumerate(moves):
            halo.append(
                rcp(
                    src_ref=src, dst_ref=hal.at[d, pl.ds(start, size)],
                    send_sem=h_send.at[d, s], recv_sem=h_recv.at[d, s],
                    device_id=to, device_id_type=MESH,
                )
            )

    def polar_copy(step, d):
        to = lax.rem(lon + step, n)
        buf, rows = ((polf, FROWS * nl), (polc, CROWS * nl))[d]
        return rcp(
            src_ref=srcs[d].at[pl.ds(0, rows)], dst_ref=buf.at[lon],
            send_sem=p_send.at[d, step], recv_sem=p_recv.at[d, step],
            device_id=(part, lat, to), device_id_type=MESH,
        )

    def bias_copy(step):
        to = lax.rem(mine + step, 2 * n)
        return rcp(
            src_ref=bsend, dst_ref=brecv.at[mine],
            send_sem=b_ssem.at[step], recv_sem=b_rsem.at[step],
            device_id=(part, to // n, lax.rem(to, n)), device_id_type=MESH,
        )

    def loop(lo, hi, body):
        def run(i, _):
            body(i)
            return 0

        lax.fori_loop(lo, hi, run, 0)

    for c in halo:
        c.start()

    @pl.when(lat == 0)
    def _():
        loop(1, n, lambda step: [polar_copy(step, d).start() for d in range(2)])
        polf[lon] = x_ref[0 : FROWS * nl, :]
        polc[lon] = g_ref[0 : CROWS * nl, :]

    loop(1, 2 * n, lambda step: bias_copy(step).start())
    brecv[mine] = bsend[...]

    def taps(b, rs, ls, qs, width):
        rid = lax.broadcasted_iota(jnp.int32, (m, width), 0)
        j = lax.rem(rid, nl)
        i = lax.rem(rid // nl, BR) + b * BR
        dr = rs - i + 1
        dl = ls - j + 1
        ok = (dr >= 0) & (dr < 3) & (dl >= 0) & (dl < 3)
        code = jnp.where(ok, dr * 3 + dl, -1)
        start = b * m if isinstance(b, int) else pl.multiple_of(b * m, m)
        coefs = p_ref[pl.ds(start, m), :]
        fwd = jnp.zeros((m, width), F32)
        bwd = jnp.zeros((m, width), F32)
        for q in qs:
            hit = code == q
            fwd = jnp.where(hit, coefs[:, q : q + 1], fwd)
            bwd = jnp.where(hit, coefs[:, 17 - q : 18 - q], bwd)
        return fwd.astype(BF16), bwd.astype(BF16)

    def window(b):
        return jnp.clip(b * BR - 4, 0, nrow - 16)

    def build(b):
        lane = lax.broadcasted_iota(jnp.int32, (m, 16 * nl), 1)
        a_own[0, b], a_own[1, b] = taps(
            b, window(b) + lane // nl, lax.rem(lane, nl), range(9), 16 * nl
        )
        lane = lax.broadcasted_iota(jnp.int32, (m, 2 * nrow), 1)
        a_lr[0, b], a_lr[1, b] = taps(
            b, lax.rem(lane, nrow), jnp.where(lane < nrow, -1, nl), (0, 2, 3, 5, 6, 8), 2 * nrow
        )

    loop(0, nb, build)
    lane = lax.broadcasted_iota(jnp.int32, (m, 48), 1)
    rs = jnp.where(
        lane < 32,
        lax.rem(lane, 16) + jnp.where(lat == 0, nrow, -16),
        (lane - 32) // nl + jnp.where(lat == 0, nrow, -16 // nl),
    )
    ls = jnp.where(lane < 16, -1, jnp.where(lane < 32, nl, lax.rem(lane, nl)))
    a_t[0], a_t[1] = taps(other * (nb - 1), rs, ls, range(9), 48)

    tr = kk * BR

    @pl.when(lat == 0)
    def _():
        rid = lax.broadcasted_iota(jnp.int32, (m, m), 0)
        cid = lax.broadcasted_iota(jnp.int32, (m, m), 1)
        order = ((rid // nl == lax.rem(cid, tr)) & (lax.rem(rid, nl) == cid // tr)).astype(BF16)
        for d, rows in ((0, FROWS), (1, CROWS)):
            wide = GROUP * rows * nl

            def far_group(grp, d=d, rows=rows, wide=wide):
                lane = lax.broadcasted_iota(jnp.int32, (circle, wide), 1)
                t_id = lax.broadcasted_iota(jnp.int32, (circle, wide), 0)
                lon_of = (grp * GROUP + lane // (rows * nl)) * nl + lax.rem(lane, nl)
                rlane = lax.broadcasted_iota(jnp.int32, (tr, wide), 1)
                r_of = lax.rem(rlane // nl, rows)
                i_of = lax.rem(lax.broadcasted_iota(jnp.int32, (tr, wide), 0), BR)
                dist = lon_of - lon * nl + circle
                for j in range(nl):
                    if d == 0:
                        t_want = lax.rem(dist - j + circle, circle)
                    else:
                        t_want = lax.rem(2 * circle - dist + j + circle, circle)
                    pick = (t_id == t_want).astype(BF16)
                    full = dot(t_ref[d * 3 * tr : (d + 1) * 3 * tr, :], pick)
                    acc = jnp.zeros((tr, wide), F32)
                    for w in range(3):
                        hit = (r_of - i_of + 1 == w) if d == 0 else (i_of - r_of + 1 == w)
                        acc = jnp.where(hit, full[w * tr : (w + 1) * tr], acc)
                    a_j[j * tr : (j + 1) * tr, 0:wide] = acc.astype(BF16)
                dst = a_farf if d == 0 else a_farc
                dst[grp] = dot(order, a_j[:, 0:wide]).astype(BF16)

            loop(0, n // GROUP, far_group)

    def near(d, b):
        start = window(b) * nl
        start = pl.multiple_of(start, 16)
        return dot(a_own[d, b], srcs[d][pl.ds(start, 16 * nl), :]) + dot(
            a_lr[d, b], hal[d, 0 : 2 * nrow, :]
        )

    def put(d, b, acc):
        at = pl.multiple_of(b * cells, cells)
        for k in range(kk):
            zs[d, k, pl.ds(at, cells), :] = acc[k * cells : (k + 1) * cells].astype(BF16)

    def inner(d):
        loop(1, nb - 1, lambda b: put(d, b, near(d, b)))

    def edges(d):
        edge_acc[0] = near(d, jnp.int32(0))
        edge_acc[1] = near(d, jnp.int32(nb - 1))
        edge_acc[other] += dot(a_t[d], hal[d, 2 * nrow : 2 * nrow + 48, :])

        @pl.when(lat == 0)
        def _():
            loop(1, n, lambda step: polar_copy(step, d).wait())
            buf, coefs, rows = ((polf, a_farf, FROWS), (polc, a_farc, CROWS))[d]

            def far_add(grp):
                src = buf[pl.ds(grp * GROUP, GROUP)].reshape(GROUP * rows * nl, chan)
                edge_acc[0] += dot(coefs[grp], src)

            loop(0, n // GROUP, far_add)

        put(d, jnp.int32(0), edge_acc[0])
        put(d, jnp.int32(nb - 1), edge_acc[1])

    for c in halo:
        c.wait()
    inner(0)
    edges(0)

    def copy0(k):
        return rcp(
            src_ref=s0.at[k], dst_ref=r0.at[k], send_sem=send0.at[k], recv_sem=recv0.at[k],
            device_id=(part, other, lon), device_id_type=MESH,
        )

    def copy1(k):
        return rcp(
            src_ref=s1.at[k], dst_ref=r1.at[k], send_sem=send1.at[k], recv_sem=recv1.at[k],
            device_id=(part, lat, lon + 1 - 2 * par), device_id_type=MESH,
        )

    def copy2(k, step):
        to = lax.rem(zz + step, nz)
        return rcp(
            src_ref=s2.at[k, to], dst_ref=r2.at[k, zz],
            send_sem=send2.at[k, step], recv_sem=recv2.at[k, step],
            device_id=(part, lat, to * 2 + par), device_id_type=MESH,
        )

    def grads(k, which):
        z = zs[0, k, :, pl.ds(pl.multiple_of(which * half, half), half)]
        return lax.dot_general(
            z, g_ref[...], (((0,), (0,)), ((), ())), preferred_element_type=F32
        )

    def stage0(k):
        s0[k] = grads(k, other).astype(BF16)
        copy0(k).start()

    def keep(k):
        own[k] = grads(k, lat).reshape(own.shape[1:])

    loop(0, kk, stage0)
    loop(0, kk, keep)

    def stage1(k):
        copy0(k).wait()
        own[k] += r0[k].astype(F32).reshape(own.shape[1:])
        for q in range(nz):
            s1[k, q] = own[k, q, 1 - par].astype(BF16)
        copy1(k).start()

    loop(0, kk, stage1)

    step_rows = 256

    def forward(b):
        at = pl.ds(pl.multiple_of(b * step_rows, step_rows), step_rows)
        acc = dot(zs[0, 0, at, :], w_ref[0])
        for k in range(1, kk):
            acc += dot(zs[0, k, at, :], w_ref[k])
        out_ref[at, :] = (acc + b_ref[...]).astype(BF16)

    loop(0, nrow * nl // step_rows, forward)

    def stage2(k):
        copy1(k).wait()
        for q in range(nz):
            own[k, q, par] += r1[k, q].astype(F32)
            s2[k, q] = own[k, q, par].astype(BF16)
        loop(1, nz, lambda step: copy2(k, step).start())

    loop(0, kk, stage2)

    inner(1)
    edges(1)

    def backward(b):
        at = pl.ds(pl.multiple_of(b * step_rows, step_rows), step_rows)
        acc = None
        for k in range(kk):
            term = lax.dot_general(
                zs[1, k, at, :], w_ref[k], (((1,), (1,)), ((), ())), preferred_element_type=F32
            )
            acc = term if acc is None else acc + term
        gf_ref[at, :] = acc.astype(BF16)

    loop(0, nrow * nl // step_rows, backward)

    loop(1, 2 * n, lambda step: bias_copy(step).wait())
    gb_ref[...] = jnp.sum(brecv[...], axis=0) * scale

    def final(k):
        gw_ref[k] = own[k, zz, par]

        def take(step):
            copy2(k, step).wait()
            gw_ref[k] += r2[k, lax.rem(zz + nz - step, nz)].astype(F32)

        loop(1, nz, take)
        gw_ref[k] = gw_ref[k] * scale

    loop(0, kk, final)


def on_device(fields, psi_near, psi_far, blocks, weight, out_bias, cotangent):
    nrow, nl, chan = fields.shape
    kk = weight.shape[0]
    npol, ns, _, _, bw = psi_far.shape
    n = lax.axis_size("lon")
    circle = n * nl
    lat = lax.axis_index("lat")
    nb = nrow // BR
    m = BR * nl * kk

    psi_pad = jnp.pad(psi_near, ((1, 1), (0, 0), (0, 0), (0, 0)))
    psi = lax.dynamic_slice_in_dim(psi_pad, lat * nrow, nrow + 2, 0)
    own_rows = psi[1 : nrow + 1].reshape(nrow, kk, 9)
    back = [psi[2 - w : 2 - w + nrow, :, w] for w in range(3)]
    both = jnp.concatenate([own_rows] + back, axis=2)
    both = both.reshape(nb, BR, kk, 18).transpose(0, 2, 1, 3).astype(F32)
    coefs = jnp.broadcast_to(both[:, :, :, None, :], (nb, kk, BR, nl, 18)).reshape(nb * m, 18)

    ids = jnp.arange(circle // bw, dtype=jnp.int32)
    picker = (blocks[:, :, None] == ids).astype(BF16)
    table = jnp.einsum("psb,pskwe->wkpbe", picker, psi_far, preferred_element_type=F32)
    table = table.reshape(3, kk, npol, circle).astype(BF16)
    tf = jnp.pad(table, ((0, 0), (0, 0), (0, BR - npol), (0, 0)))
    wide = jnp.pad(table, ((0, 0), (0, 0), (1, BR), (0, 0)))
    tb = jnp.stack([wide[w, :, 2 - w : 2 - w + BR] for w in range(3)])
    tables = jnp.concatenate([tf, tb]).reshape(6 * kk * BR, circle)

    edge_cols = jnp.stack([fields[:, 0], fields[:, nl - 1], cotangent[:, 0], cotangent[:, nl - 1]])
    lat_count = lax.axis_size("lat")
    scale = 1.0 / math.sqrt(nrow * lat_count * circle)
    nz = n // 2
    cr = chan // 2 // n
    vmem = pl.BlockSpec(memory_space=pltpu.VMEM)
    dma = pltpu.SemaphoreType.DMA
    ng = n // GROUP
    out, gf, gw, gb = pl.pallas_call(
        functools.partial(kernel, n, nrow, nl, kk, scale),
        out_shape=(
            jax.ShapeDtypeStruct((nrow * nl, chan), BF16),
            jax.ShapeDtypeStruct((nrow * nl, chan), BF16),
            jax.ShapeDtypeStruct((kk, cr, chan), F32),
            jax.ShapeDtypeStruct((8, chan), F32),
        ),
        in_specs=[vmem] * 7,
        out_specs=(vmem,) * 4,
        scratch_shapes=[
            pltpu.VMEM((2, 2 * nrow + 48, chan), BF16),
            pltpu.VMEM((n, FROWS * nl, chan), BF16),
            pltpu.VMEM((n, CROWS * nl, chan), BF16),
            pltpu.VMEM((2, nb, m, 16 * nl), BF16),
            pltpu.VMEM((2, nb, m, 2 * nrow), BF16),
            pltpu.VMEM((2, m, 48), BF16),
            pltpu.VMEM((m, GROUP * FROWS * nl), BF16),
            pltpu.VMEM((ng, m, GROUP * FROWS * nl), BF16),
            pltpu.VMEM((ng, m, GROUP * CROWS * nl), BF16),
            pltpu.VMEM((2, kk, nrow * nl, chan), BF16),
            pltpu.VMEM((2, m, chan), F32),
            pltpu.VMEM((kk, chan // 2, chan), BF16),
            pltpu.VMEM((kk, chan // 2, chan), BF16),
            pltpu.VMEM((kk, nz, 2, cr, chan), F32),
            pltpu.VMEM((kk, nz, cr, chan), BF16),
            pltpu.VMEM((kk, nz, cr, chan), BF16),
            pltpu.VMEM((kk, nz, cr, chan), BF16),
            pltpu.VMEM((kk, nz, cr, chan), BF16),
            pltpu.VMEM((8, chan), F32),
            pltpu.VMEM((2 * n, 8, chan), F32),
            dma((2, 5)), dma((2, 5)),
            dma((2, n)), dma((2, n)),
            dma((kk,)), dma((kk,)),
            dma((kk,)), dma((kk,)),
            dma((kk, nz)), dma((kk, nz)),
            dma((2 * n,)), dma((2 * n,)),
        ],
        compiler_params=pltpu.CompilerParams(
            collective_id=0, has_side_effects=True, vmem_limit_bytes=56 * 1024 * 1024
        ),
        cost_estimate=pl.CostEstimate(
            flops=8 * nrow * nl * kk * chan * chan, bytes_accessed=8 << 20, transcendentals=0
        ),
    )(
        fields.reshape(nrow * nl, chan),
        cotangent.reshape(nrow * nl, chan),
        edge_cols, coefs, tables, weight, out_bias.reshape(1, chan),
    )
    place = lat * n + lax.axis_index("lon")
    share = chan // (lat_count * n)
    grad_bias = lax.dynamic_slice_in_dim(gb[0], place * share, share, 0)
    return (out.reshape(fields.shape), gf.reshape(fields.shape), gw, grad_bias)


def solution(mesh):
    return jax.shard_map(
        on_device,
        mesh=mesh,
        in_specs=(
            P(("parts", "lat"), "lon", None), P(), P(), P(), P(), P(),
            P(("parts", "lat"), "lon", None),
        ),
        out_specs=(
            P(("parts", "lat"), "lon", None),
            P(("parts", "lat"), "lon", None),
            P(None, ("parts", "lat", "lon"), None),
            P(("parts", "lat", "lon")),
        ),
        check_vma=False,
    )
```

time: 189 us -> 62.1 us (0.33); the launches traced: 186 us -> 61.7 us
  blocking collectives: 62.7 us -> 0 us
  local copies, waits for them, and re-layouts: 63.1 us -> 12.6 us
  Pallas kernels: 0 us -> 46.6 us
  matrix products: 25.8 us -> 0.29 us
  between operations: 15.1 us -> 0.76 us
  other arithmetic: 11.9 us -> 1.5 us
  starting transfers between devices: 4.72 us -> 0 us
  waiting for transfers between devices: 2.5 us -> 0 us
    pallas_call x0 -> x1, Pallas kernels: none -> 46.6 us  [on_device(): pl.pallas_call(functools.partial(kernel, n, nrow, nl, kk, scale), out_sha...]
    all_gather x1 -> x0, blocking collectives: 32.8 us -> none  [on_device(): shard_piece = lax.all_gather(polar_fields, 'lon', axis=1, tiled=True)]
    unnamed x1 -> x0, blocking collectives: 29.9 us -> none
    slice x8 -> x6, local copies, waits for them, and re-layouts: 33.8 us -> 3.94 us  [the longest x1 1.41 us: on_device(): fields[:, 0]]
    dot_general x20 -> x1, matrix products: 25.8 us -> 0.29 us  [on_device(): jnp.einsum('psb,pskwe->wkpbe', picker, psi_far, preferred_element_type=F32)]
    squeeze x4 -> x0, local copies, waits for them, and re-layouts: 7.65 us -> none  [on_device(): near_band[:, :, tap_row]]
    gather x2 -> x0, local copies, waits for them, and re-layouts: 6.59 us -> none  [far_coeffs(): return jnp.take(dense_table, distance, axis=3)]
    ppermute x3 -> x0, starting transfers between devices: 4.64 us -> none  [the longest x1 4.12 us: with_halo(): lax.ppermute(lax.slice_in_dim(block, 0, width, axis=dim), axis, backward)]
  transfers between devices with their start and end apart: 5 -> 0, of which waited for: 1 -> 0; matrix products, arithmetic and copies ran while one was open for 50% -> 0% of each run, Pallas kernels for 0% -> 0%
where the time goes in v1:
time: 62.1 us; the launch traced here: 61.7 us
  Pallas kernels  46.6 us (75%)
  local copies, waits for them, and re-layouts  12.6 us (20%)
  other arithmetic  1.5 us (2%)
  between operations  0.76 us (1%)
    pallas_call x1, Pallas kernels, on_device(): pl.pallas_call(functools.partial(kernel, n, nrow, nl, kk, scale), out_sha...  46.6 us
    unnamed x10, local copies, waits for them, and re-layouts  5.28 us
    concatenate x8, local copies, waits for them, and re-layouts, on_device(): both = jnp.concatenate([own_rows] + back, axis=2)  1.52 us
    slice x1, local copies, waits for them, and re-layouts, on_device(): fields[:, 0]  1.41 us

profile of v1, /device:TPU:0, one launch (start us, length us, event | category | flops | bytes accessed | tf_op | source)
XLA Modules:
  0.0 61.7 jit_solution(7600162170674322227)
XLA Ops:
  0.6 0.0 copy-start
  0.6 0.0 copy-start.2
  0.7 0.8 %copy.44 = s32[4,2]{1,0:T(4,128)S(1)} copy(s32[4,2]{0,1:T(2,128)} %param.10) | data formatting | bytes 64 | tf_op args[3]
  1.5 0.8 %pad_dynamic-slice_fusion.1 = (bf16[64,4,1,3]{0,1,3,2:T(4,128)(2,1)S(1)}, bf16[64,4,1,3]{0,1,3,2:T(4,128)(2,1)S(1)}, bf16[64,4,1,3]{0,1,3,2:T(4,128)(2,1)S(1)}) fusion(s32[]{:T(128)S(6)} %add.19, bf16[128,4,3,3]{0,1,3,2:T(4,128)(2,1)} %param.8, s32[]{:T(128)S(6)} %add.18, s32[]{:T(128)S(6)} %add.21, s32[]{:T(128)S(6)} %select_n.6, s32[]{:T(128)S(6)} %add.22), kind=kLoop, calls=%fused_computation.18 | loop fusion | bytes 13844 | tf_op jit(solution)/shard_map/slice | solution.py:348
  2.3 0.8 %pad_dynamic-slice_fusion.2 = bf16[64,4,3,3]{0,1,3,2:T(4,128)(2,1)S(1)} fusion(s32[]{:T(128)S(6)} %add.18, bf16[128,4,3,3]{0,1,3,2:T(4,128)(2,1)} %param.8), kind=kLoop, calls=%fused_computation.19 | loop fusion | bytes 13828 | tf_op jit(solution)/shard_map/slice | solution.py:347
  3.1 0.1 concatenate.16
  3.2 0.1 concatenate.17
  3.3 0.1 concatenate.18
  3.3 0.3 copy.43
  3.6 0.3 copy.42
  3.9 0.3 copy.41
  4.2 0.0 copy-done
  4.2 0.3 fusion
  4.5 0.1 reshape.52
  4.6 0.6 %fusion.4 = bf16[6,4,8,64]{3,2,1,0:T(8,128)(2,1)} fusion(bf16[3,4,4,64]{3,2,1,0:T(4,128)(2,1)S(1)} %copy.48, bf16[1,4,8,64]{3,2,1,0:T(8,128)(2,1)S(1)} %get-tuple-element.18, bf16[1,4,8,64]{3,2,1,0:T(8,128)(2,1)S(1)} %get-tuple-element.17, bf16[1,4,8,64]{3,2,1,0:T(8,128)(2,1)S(1)} %get-tuple-element.16), kind=kLoop, calls=%fused_computation.15 | loop fusion | flops 122880 | bytes 43008 | tf_op jit(solution)/shard_map/concatenate | solution.py:360
  5.3 0.1 concatenate.15
  5.4 0.3 copy.40
  5.7 0.1 convert_bitcast_fusion
  5.8 1.4 %fusion.11 = (bf16[64,1,512]{2,1,0:T(2,128)(2,1)S(1)}, bf16[64,1,512]{2,1,0:T(2,128)(2,1)S(1)}) fusion(bf16[64,8,512]{2,1,0:T(8,128)(2,1)} %param.7), kind=kLoop, calls=%fused_computation.27 | loop fusion | bytes 262144 | tf_op jit(solution)/shard_map/slice | solution.py:362
  7.3 0.0 copy-done.2
  7.3 0.2 fusion.12
  7.5 0.7 %pad_maximum_fusion.e_ref = bf16[4,64,512]{2,1,0:T(8,128)(2,1)} fusion(bf16[1,64,512]{2,1,0:T(8,128)(2,1)S(1)} %get-tuple-element.22, bf16[1,64,512]{2,1,0:T(8,128)(2,1)S(1)} %get-tuple-element.23, bf16[1,64,512]{2,1,0:T(8,128)(2,1)S(1)} %get-tuple-element.24, bf16[1,64,512]{2,1,0:T(8,128)(2,1)S(1)} %get-tuple-element.25), kind=kLoop, calls=%fused_computation.2 | loop fusion | flops 393216 | bytes 524288 | tf_op jit(solution)/shard_map/stack | solution.py:362
  8.2 1.1 %broadcast_in_dim.2 = f32[8,4,8,8,18]{4,3,2,1,0:T(8,128)} broadcast(f32[8,4,8,18]{3,2,1,0:T(8,128)S(1)} %convert_bitcast_fusion), dimensions={0,1,2,4} | broadcast | bytes 165888 | tf_op jit(solution)/shard_map/broadcast_in_dim | solution.py:351
  9.3 46.6 %shard_map.102 = (bf16[512,512]{1,0:T(8,128)(2,1)}, bf16[512,512]{1,0:T(8,128)(2,1)}, f32[4,32,512]{2,1,0:T(8,128)}, f32[8,512]{1,0:T(8,128)}) custom-call(bf16[512,512]{1,0:T(8,128)(2,1)} %bitcast.39, bf16[512,512]{1,0:T(8,128)(2,1)} %bitcast.40, bf16[4,64,512]{2,1,0:T(8,128)(2,1)} %pad_maximum_fusion.e_ref, f32[2048,18]{1,0:T(8,128)} %bitcast.36, ...), custom_call_target="tpu_custom_call" | custom-call | flops 4294967296 | bytes 8388608 | tf_op jit(solution)/shard_map/pallas_call | solution.py:370
  55.9 0.0 copy-start.1
  55.9 0.8 %slice.47 = f32[1,512]{1,0:T(1,128)S(1)} slice(f32[8,512]{1,0:T(8,128)} %get-tuple-element.11), slice={[0:1], [0:512]} | slice | bytes 4096 | tf_op jit(solution)/shard_map/slice | solution.py:421
  56.7 0.6 fusion.10
  57.3 1.9 %copy.62 = bf16[64,8,512]{2,1,0:T(8,128)(2,1)} copy(bf16[64,8,512]{2,1,0:T(8,128)(2,1)} %bitcast.38) | data formatting | bytes 1048576
  59.1 1.9 %copy.63 = bf16[64,8,512]{2,1,0:T(8,128)(2,1)} copy(bf16[64,8,512]{2,1,0:T(8,128)(2,1)} %bitcast.37) | data formatting | bytes 1048576
  61.0 0.0 copy-done.1
  61.0 0.7 %copy.64 = f32[4,32,512]{2,1,0:T(8,128)} copy(f32[4,32,512]{2,1,0:T(8,128)S(1)} %copy-done.1) | data formatting | bytes 524288
  (4 shorter events, 0.1 us)
Async XLA Ops:
  0.6 3.6 %copy-start = (bf16[4,2,4,3,16]{4,2,3,1,0:T(4,128)(2,1)S(1)}, bf16[4,2,4,3,16]{4,2,3,1,0:T(4,128)(2,1)}, u32[]{:S(2)}) copy-start(bf16[4,2,4,3,16]{4,2,3,1,0:T(4,128)(2,1)} %param.9) | copy-start | bytes 9220
  0.6 6.6 %copy-start.2 = (bf16[64,8,512]{2,1,0:T(8,128)(2,1)S(1)}, bf16[64,8,512]{2,1,0:T(8,128)(2,1)}, u32[]{:S(2)}) copy-start(bf16[64,8,512]{2,1,0:T(8,128)(2,1)} %param.13) | copy-start | bytes 1572868
  55.9 5.1 %copy-start.1 = (f32[4,32,512]{2,1,0:T(8,128)S(1)}, f32[4,32,512]{2,1,0:T(8,128)}, u32[]{:S(2)}) copy-start(f32[4,32,512]{2,1,0:T(8,128)} %get-tuple-element.32) | copy-start | bytes 786436

commit v2 on v1

--- a/solution.py
+++ b/solution.py
@@ -23,8 +23,9 @@
 
 def kernel(
     n, nrow, nl, kk, scale,
-    x_ref, g_ref, e_ref, p_ref, t_ref, w_ref, b_ref,
-    out_ref, gf_ref, gw_ref, gb_ref,
+    x_ref, g_ref, psi_ref, far_ref, blk_ref, w_hbm, b_ref,
+    out_hbm, gf_hbm, gw_ref, gb_ref,
+    w_ref, out_ref, gf_ref, ecols, t_ref, loc_sem,
     hal, polf, polc, a_own, a_lr, a_t, a_j, a_farf, a_farc, zs, edge_acc,
     s0, r0, own, s1, r1, s2, r2, bsend, brecv,
     h_send, h_recv, p_send, p_recv, send0, recv0, send1, recv1, send2, recv2, b_ssem, b_rsem,
@@ -46,6 +47,10 @@
     zz = lon // 2
     nz = n // 2
     rcp = pltpu.make_async_remote_copy
+    load_w = pltpu.make_async_copy(w_hbm, w_ref, loc_sem.at[0])
+    store_out = pltpu.make_async_copy(out_ref, out_hbm, loc_sem.at[1])
+    store_gf = pltpu.make_async_copy(gf_ref, gf_hbm, loc_sem.at[2])
+    load_w.start()
 
     barrier = pltpu.get_barrier_semaphore()
 
@@ -60,6 +65,14 @@
     bsend[...] = jnp.broadcast_to(
         jnp.sum(g_ref[...].astype(F32), axis=0, keepdims=True), bsend.shape
     )
+    rid = lax.broadcasted_iota(jnp.int32, (2 * nrow, nrow * nl), 0)
+    cid = lax.broadcasted_iota(jnp.int32, (2 * nrow, nrow * nl), 1)
+    want = lax.rem(rid, nrow) * nl + jnp.where(rid < nrow, 0, nl - 1)
+    ends = (cid == want).astype(BF16)
+    for d, src in enumerate((x_ref, g_ref)):
+        picked = dot(ends, src[...]).astype(BF16)
+        ecols[2 * d] = picked[:nrow]
+        ecols[2 * d + 1] = picked[nrow:]
     pl.semaphore_wait(barrier, 2 * n - 1)
 
     srcs = (x_ref, g_ref)
@@ -67,8 +80,8 @@
     cell_cut = pl.multiple_of(other * (nrow * nl - 16), 16)
     halo = []
     for d in range(2):
-        first = e_ref.at[2 * d]
-        last = e_ref.at[2 * d + 1]
+        first = ecols.at[2 * d]
+        last = ecols.at[2 * d + 1]
         moves = (
             (last, 0, nrow, (part, lat, right)),
             (first, nrow, nrow, (part, lat, left)),
@@ -121,46 +134,66 @@
     loop(1, 2 * n, lambda step: bias_copy(step).start())
     brecv[mine] = bsend[...]
 
-    def taps(b, rs, ls, qs, width):
-        rid = lax.broadcasted_iota(jnp.int32, (m, width), 0)
-        j = lax.rem(rid, nl)
-        i = lax.rem(rid // nl, BR) + b * BR
-        dr = rs - i + 1
-        dl = ls - j + 1
+    nlat = psi_ref.shape[1]
+
+    def psi_rows(b):
+        rid = lax.broadcasted_iota(jnp.int32, (3 * cells, nlat), 0)
+        cid = lax.broadcasted_iota(jnp.int32, (3 * cells, nlat), 1)
+        want = lat * nrow + b * BR + lax.rem(rid, cells) // nl + 1 - rid // cells
+        return lax.dot_general(
+            (cid == want).astype(BF16), psi_ref[...], (((1,), (1,)), ((), ())),
+            preferred_element_type=F32,
+        )
+
+    def taps(b, pv, rs, ls, qs, dst):
+        width = rs.shape[1]
+        rid = lax.broadcasted_iota(jnp.int32, (cells, width), 0)
+        dr = rs - (rid // nl + b * BR) + 1
+        dl = ls - lax.rem(rid, nl) + 1
         ok = (dr >= 0) & (dr < 3) & (dl >= 0) & (dl < 3)
         code = jnp.where(ok, dr * 3 + dl, -1)
-        start = b * m if isinstance(b, int) else pl.multiple_of(b * m, m)
-        coefs = p_ref[pl.ds(start, m), :]
-        fwd = jnp.zeros((m, width), F32)
-        bwd = jnp.zeros((m, width), F32)
-        for q in qs:
-            hit = code == q
-            fwd = jnp.where(hit, coefs[:, q : q + 1], fwd)
-            bwd = jnp.where(hit, coefs[:, 17 - q : 18 - q], bwd)
-        return fwd.astype(BF16), bwd.astype(BF16)
+        for d in range(2):
+            for k in range(kk):
+                vals = jnp.zeros((cells, width), F32)
+                for q in qs:
+                    w, at = (1, q * kk + k) if d == 0 else (2 - q // 3, (8 - q) * kk + k)
+                    col = pv[w * cells : (w + 1) * cells, at : at + 1]
+                    vals = jnp.where(code == q, col, vals)
+                dst(d, k, vals.astype(BF16))
 
     def window(b):
         return jnp.clip(b * BR - 4, 0, nrow - 16)
 
     def build(b):
-        lane = lax.broadcasted_iota(jnp.int32, (m, 16 * nl), 1)
-        a_own[0, b], a_own[1, b] = taps(
-            b, window(b) + lane // nl, lax.rem(lane, nl), range(9), 16 * nl
-        )
-        lane = lax.broadcasted_iota(jnp.int32, (m, 2 * nrow), 1)
-        a_lr[0, b], a_lr[1, b] = taps(
-            b, lax.rem(lane, nrow), jnp.where(lane < nrow, -1, nl), (0, 2, 3, 5, 6, 8), 2 * nrow
+        pv = psi_rows(b)
+
+        def put_own(d, k, vals):
+            a_own[d, b, k * cells : (k + 1) * cells, :] = vals
+
+        def put_lr(d, k, vals):
+            a_lr[d, b, k * cells : (k + 1) * cells, :] = vals
+
+        lane = lax.broadcasted_iota(jnp.int32, (cells, 16 * nl), 1)
+        taps(b, pv, window(b) + lane // nl, lax.rem(lane, nl), range(9), put_own)
+        lane = lax.broadcasted_iota(jnp.int32, (cells, 2 * nrow), 1)
+        taps(
+            b, pv, lax.rem(lane, nrow), jnp.where(lane < nrow, -1, nl), (0, 2, 3, 5, 6, 8), put_lr
         )
 
     loop(0, nb, build)
-    lane = lax.broadcasted_iota(jnp.int32, (m, 48), 1)
+    lane = lax.broadcasted_iota(jnp.int32, (cells, 48), 1)
     rs = jnp.where(
         lane < 32,
         lax.rem(lane, 16) + jnp.where(lat == 0, nrow, -16),
         (lane - 32) // nl + jnp.where(lat == 0, nrow, -16 // nl),
     )
     ls = jnp.where(lane < 16, -1, jnp.where(lane < 32, nl, lax.rem(lane, nl)))
-    a_t[0], a_t[1] = taps(other * (nb - 1), rs, ls, range(9), 48)
+
+    def put_t(d, k, vals):
+        a_t[d, k * cells : (k + 1) * cells, :] = vals
+
+    eb = other * (nb - 1)
+    taps(eb, psi_rows(eb), rs, ls, range(9), put_t)
 
     tr = kk * BR
 
@@ -168,6 +201,23 @@
     def _():
         rid = lax.broadcasted_iota(jnp.int32, (m, m), 0)
         cid = lax.broadcasted_iota(jnp.int32, (m, m), 1)
+        frows, bw = far_ref.shape
+        npol, ns = blk_ref.shape
+        lane = lax.broadcasted_iota(jnp.int32, (bw, circle), 1)
+        spread = (lax.broadcasted_iota(jnp.int32, (bw, circle), 0) == lax.rem(lane, bw)).astype(BF16)
+        frow = lax.broadcasted_iota(jnp.int32, (frows, circle), 0) // (3 * kk)
+        block = jnp.zeros((frows, circle), jnp.int32)
+        for q in range(npol * ns):
+            block = jnp.where(frow == q, blk_ref[q // ns, q % ns], block)
+        lane = lax.broadcasted_iota(jnp.int32, (frows, circle), 1)
+        named = jnp.where(block == lane // bw, dot(far_ref[...], spread), 0.0).astype(BF16)
+        trow = lax.broadcasted_iota(jnp.int32, (6 * tr, frows), 0)
+        srow = lax.broadcasted_iota(jnp.int32, (6 * tr, frows), 1)
+        t_i = lax.rem(trow, BR)
+        t_wk = lax.rem(trow, 3 * tr) // BR
+        t_p = jnp.where(trow < 3 * tr, t_i, t_i - t_wk // kk + 1)
+        pick_row = (lax.rem(srow, 3 * kk) == t_wk) & (srow // (3 * kk * ns) == t_p)
+        t_ref[...] = dot(pick_row.astype(BF16), named).astype(BF16)
         order = ((rid // nl == lax.rem(cid, tr)) & (lax.rem(rid, nl) == cid // tr)).astype(BF16)
         for d, rows in ((0, FROWS), (1, CROWS)):
             wide = GROUP * rows * nl
@@ -290,7 +340,9 @@
             acc += dot(zs[0, k, at, :], w_ref[k])
         out_ref[at, :] = (acc + b_ref[...]).astype(BF16)
 
+    load_w.wait()
     loop(0, nrow * nl // step_rows, forward)
+    store_out.start()
 
     def stage2(k):
         copy1(k).wait()
@@ -315,6 +367,7 @@
         gf_ref[at, :] = acc.astype(BF16)
 
     loop(0, nrow * nl // step_rows, backward)
+    store_gf.start()
 
     loop(1, 2 * n, lambda step: bias_copy(step).wait())
     gb_ref[...] = jnp.sum(brecv[...], axis=0) * scale
@@ -330,6 +383,26 @@
         gw_ref[k] = gw_ref[k] * scale
 
     loop(0, kk, final)
+    store_out.wait()
+    store_gf.wait()
+
+
+def hand_on(n, out_in, gf_in, gw_in, gb_in, out_ref, gf_ref, gw_ref, gb_ref, sem):
+    copies = []
+    for a, (src, dst) in enumerate(((out_in, out_ref), (gf_in, gf_ref), (gw_in, gw_ref))):
+        count = sem.shape[1]
+        size = src.shape[0] // count
+        for c in range(count):
+            at = pl.ds(c * size, size)
+            copies.append(pltpu.make_async_copy(src.at[at], dst.at[at], sem.at[a, c]))
+    for c in copies:
+        c.start()
+    share = gb_ref.shape[1]
+    chan = gb_in.shape[1]
+    place = lax.axis_index("lat") * n + lax.axis_index("lon")
+    gb_ref[...] = pltpu.roll(gb_in[...], lax.rem(chan - place * share, chan), 1)[0:1, :share]
+    for c in copies:
+        c.wait()
 
 
 def on_device(fields, psi_near, psi_far, blocks, weight, out_bias, cotangent):
@@ -338,33 +411,16 @@
     npol, ns, _, _, bw = psi_far.shape
     n = lax.axis_size("lon")
     circle = n * nl
-    lat = lax.axis_index("lat")
     nb = nrow // BR
     m = BR * nl * kk
-
-    psi_pad = jnp.pad(psi_near, ((1, 1), (0, 0), (0, 0), (0, 0)))
-    psi = lax.dynamic_slice_in_dim(psi_pad, lat * nrow, nrow + 2, 0)
-    own_rows = psi[1 : nrow + 1].reshape(nrow, kk, 9)
-    back = [psi[2 - w : 2 - w + nrow, :, w] for w in range(3)]
-    both = jnp.concatenate([own_rows] + back, axis=2)
-    both = both.reshape(nb, BR, kk, 18).transpose(0, 2, 1, 3).astype(F32)
-    coefs = jnp.broadcast_to(both[:, :, :, None, :], (nb, kk, BR, nl, 18)).reshape(nb * m, 18)
-
-    ids = jnp.arange(circle // bw, dtype=jnp.int32)
-    picker = (blocks[:, :, None] == ids).astype(BF16)
-    table = jnp.einsum("psb,pskwe->wkpbe", picker, psi_far, preferred_element_type=F32)
-    table = table.reshape(3, kk, npol, circle).astype(BF16)
-    tf = jnp.pad(table, ((0, 0), (0, 0), (0, BR - npol), (0, 0)))
-    wide = jnp.pad(table, ((0, 0), (0, 0), (1, BR), (0, 0)))
-    tb = jnp.stack([wide[w, :, 2 - w : 2 - w + BR] for w in range(3)])
-    tables = jnp.concatenate([tf, tb]).reshape(6 * kk * BR, circle)
-
-    edge_cols = jnp.stack([fields[:, 0], fields[:, nl - 1], cotangent[:, 0], cotangent[:, nl - 1]])
+    taps = psi_near.transpose(2, 3, 1, 0).reshape(9 * kk, psi_near.shape[0])
+    far = psi_far.transpose(0, 1, 3, 2, 4).reshape(npol * ns * 3 * kk, bw)
     lat_count = lax.axis_size("lat")
     scale = 1.0 / math.sqrt(nrow * lat_count * circle)
     nz = n // 2
     cr = chan // 2 // n
     vmem = pl.BlockSpec(memory_space=pltpu.VMEM)
+    anywhere = pl.BlockSpec(memory_space=pl.ANY)
     dma = pltpu.SemaphoreType.DMA
     ng = n // GROUP
     out, gf, gw, gb = pl.pallas_call(
@@ -375,9 +431,15 @@
             jax.ShapeDtypeStruct((kk, cr, chan), F32),
             jax.ShapeDtypeStruct((8, chan), F32),
         ),
-        in_specs=[vmem] * 7,
-        out_specs=(vmem,) * 4,
+        in_specs=[vmem] * 4 + [pl.BlockSpec(memory_space=pltpu.SMEM), anywhere, vmem],
+        out_specs=(anywhere, anywhere, vmem, vmem),
         scratch_shapes=[
+            pltpu.VMEM(weight.shape, BF16),
+            pltpu.VMEM((nrow * nl, chan), BF16),
+            pltpu.VMEM((nrow * nl, chan), BF16),
+            pltpu.VMEM((4, nrow, chan), BF16),
+            pltpu.VMEM((6 * kk * BR, circle), BF16),
+            dma((3,)),
             pltpu.VMEM((2, 2 * nrow + 48, chan), BF16),
             pltpu.VMEM((n, FROWS * nl, chan), BF16),
             pltpu.VMEM((n, CROWS * nl, chan), BF16),
@@ -414,12 +476,23 @@
     )(
         fields.reshape(nrow * nl, chan),
         cotangent.reshape(nrow * nl, chan),
-        edge_cols, coefs, tables, weight, out_bias.reshape(1, chan),
+        taps, far, blocks, weight, out_bias.reshape(1, chan),
     )
-    place = lat * n + lax.axis_index("lon")
     share = chan // (lat_count * n)
-    grad_bias = lax.dynamic_slice_in_dim(gb[0], place * share, share, 0)
-    return (out.reshape(fields.shape), gf.reshape(fields.shape), gw, grad_bias)
+    out, gf, gw, gb = pl.pallas_call(
+        functools.partial(hand_on, n),
+        out_shape=(
+            jax.ShapeDtypeStruct(out.shape, BF16),
+            jax.ShapeDtypeStruct(gf.shape, BF16),
+            jax.ShapeDtypeStruct(gw.shape, F32),
+            jax.ShapeDtypeStruct((1, share), F32),
+        ),
+        in_specs=[anywhere] * 3 + [vmem],
+        out_specs=(anywhere,) * 3 + (vmem,),
+        scratch_shapes=[dma((3, kk))],
+        compiler_params=pltpu.CompilerParams(vmem_limit_bytes=56 * 1024 * 1024),
+    )(out, gf, gw, gb)
+    return (out.reshape(fields.shape), gf.reshape(fields.shape), gw, gb.reshape(share))
 
 
 def solution(mesh):

time: 62.1 us -> 91.1 us (1.47)
  Pallas kernels: 46.6 us -> 87.5 us
  local copies, waits for them, and re-layouts: 12.6 us -> 2.65 us
  other arithmetic: 1.5 us -> 0 us
    pallas_call x0 -> x1, Pallas kernels: none -> 42.1 us  [on_device(): pl.pallas_call(functools.partial(hand_on, n), out_shape=(jax.ShapeDtypeSt...]
    unnamed x10 -> x1, local copies, waits for them, and re-layouts: 5.28 us -> 1.34 us
    slice x6 -> x0, local copies, waits for them, and re-layouts: 3.94 us -> none  [the longest x1 1.41 us: on_device(): fields[:, 0]]
    concatenate x8 -> x0, local copies, waits for them, and re-layouts: 1.52 us -> none  [on_device(): both = jnp.concatenate([own_rows] + back, axis=2)]
    reshape x0 -> x1, local copies, waits for them, and re-layouts: none -> 1.31 us  [on_device(): taps = psi_near.transpose(2, 3, 1, 0).reshape(9 * kk, psi_near.shape[0])]
    pallas_call x1, Pallas kernels: 46.6 us -> 45.4 us  [on_device(): pl.pallas_call(functools.partial(kernel, n, nrow, nl, kk, scale), out_sha...]
    broadcast_in_dim x1 -> x0, local copies, waits for them, and re-layouts: 1.09 us -> none  [on_device(): jnp.broadcast_to(both[:, :, :, None, :], (nb, kk, BR, nl, 18))]
where the time goes in v2:
time: 91.1 us; the launch traced here: 90.8 us
  Pallas kernels  87.5 us (96%)
  local copies, waits for them, and re-layouts  2.65 us (3%)
    pallas_call x1, Pallas kernels, on_device(): pl.pallas_call(functools.partial(kernel, n, nrow, nl, kk, scale), out_sha...  45.4 us
    pallas_call x1, Pallas kernels, on_device(): pl.pallas_call(functools.partial(hand_on, n), out_shape=(jax.ShapeDtypeSt...  42.1 us

profile of v2, /device:TPU:0, one launch (start us, length us, event | category | flops | bytes accessed | tf_op | source)
XLA Modules:
  0.0 90.8 jit_solution(16425744480464224485)
XLA Ops:
  0.6 1.3 %copy.11.blk_ref = s32[4,2]{1,0:T(4,128)} copy(s32[4,2]{0,1:T(2,128)} %param.10) | data formatting | bytes 64 | tf_op args[3]
  2.0 1.3 %reshape.34.psi_ref = bf16[36,128]{1,0:T(8,128)(2,1)} reshape(bf16[3,3,4,128]{3,2,1,0:T(4,128)(2,1)} %bitcast.10) | data formatting | bytes 18432 | tf_op jit(solution)/shard_map/reshape | solution.py:416
  3.3 45.4 %shard_map.102 = (bf16[512,512]{1,0:T(8,128)(2,1)}, bf16[512,512]{1,0:T(8,128)(2,1)}, f32[4,32,512]{2,1,0:T(8,128)}, f32[8,512]{1,0:T(8,128)}) custom-call(bf16[512,512]{1,0:T(8,128)(2,1)} %bitcast.11, bf16[512,512]{1,0:T(8,128)(2,1)} %bitcast.12, bf16[36,128]{1,0:T(8,128)(2,1)} %reshape.34.psi_ref, bf16[96,16]{1,0:T(8,128)(2,1)} %bitcast.15, ...), custom_call_target="tpu_custom_call" | custom-call | flops 4294967296 | bytes 8388608 | tf_op jit(solution)/shard_map/pallas_call | solution.py:426
  48.6 42.1 %shard_map.103 = (bf16[512,512]{1,0:T(8,128)(2,1)}, bf16[512,512]{1,0:T(8,128)(2,1)}, f32[4,32,512]{2,1,0:T(8,128)}, f32[1,32]{1,0:T(1,128)}) custom-call(bf16[512,512]{1,0:T(8,128)(2,1)} %get-tuple-element.12.out_in, bf16[512,512]{1,0:T(8,128)(2,1)} %get-tuple-element.13.gf_in, f32[4,32,512]{2,1,0:T(8,128)} %get-tuple-element.14.gw_in, ...), custom_call_target="tpu_custom_call" | custom-call | tf_op jit(solution)/shard_map/pallas_call | solution.py:482

commit v3 on v2

--- a/solution.py
+++ b/solution.py
@@ -134,14 +134,17 @@
     loop(1, 2 * n, lambda step: bias_copy(step).start())
     brecv[mine] = bsend[...]
 
-    nlat = psi_ref.shape[1]
+    nlat = psi_ref.shape[3]
+    psi = jnp.concatenate(
+        [psi_ref[w, e].astype(F32) for w in range(3) for e in range(3)], axis=0
+    ).astype(BF16)
 
     def psi_rows(b):
         rid = lax.broadcasted_iota(jnp.int32, (3 * cells, nlat), 0)
         cid = lax.broadcasted_iota(jnp.int32, (3 * cells, nlat), 1)
         want = lat * nrow + b * BR + lax.rem(rid, cells) // nl + 1 - rid // cells
         return lax.dot_general(
-            (cid == want).astype(BF16), psi_ref[...], (((1,), (1,)), ((), ())),
+            (cid == want).astype(BF16), psi, (((1,), (1,)), ((), ())),
             preferred_element_type=F32,
         )
 
@@ -202,13 +205,13 @@
         rid = lax.broadcasted_iota(jnp.int32, (m, m), 0)
         cid = lax.broadcasted_iota(jnp.int32, (m, m), 1)
         frows, bw = far_ref.shape
-        npol, ns = blk_ref.shape
+        ns, npol = blk_ref.shape
         lane = lax.broadcasted_iota(jnp.int32, (bw, circle), 1)
         spread = (lax.broadcasted_iota(jnp.int32, (bw, circle), 0) == lax.rem(lane, bw)).astype(BF16)
         frow = lax.broadcasted_iota(jnp.int32, (frows, circle), 0) // (3 * kk)
         block = jnp.zeros((frows, circle), jnp.int32)
         for q in range(npol * ns):
-            block = jnp.where(frow == q, blk_ref[q // ns, q % ns], block)
+            block = jnp.where(frow == q, blk_ref[q % ns, q // ns], block)
         lane = lax.broadcasted_iota(jnp.int32, (frows, circle), 1)
         named = jnp.where(block == lane // bw, dot(far_ref[...], spread), 0.0).astype(BF16)
         trow = lax.broadcasted_iota(jnp.int32, (6 * tr, frows), 0)
@@ -413,7 +416,7 @@
     circle = n * nl
     nb = nrow // BR
     m = BR * nl * kk
-    taps = psi_near.transpose(2, 3, 1, 0).reshape(9 * kk, psi_near.shape[0])
+    taps = psi_near.transpose(2, 3, 1, 0)
     far = psi_far.transpose(0, 1, 3, 2, 4).reshape(npol * ns * 3 * kk, bw)
     lat_count = lax.axis_size("lat")
     scale = 1.0 / math.sqrt(nrow * lat_count * circle)
@@ -476,7 +479,7 @@
     )(
         fields.reshape(nrow * nl, chan),
         cotangent.reshape(nrow * nl, chan),
-        taps, far, blocks, weight, out_bias.reshape(1, chan),
+        taps, far, blocks.T, weight, out_bias.reshape(1, chan),
     )
     share = chan // (lat_count * n)
     out, gf, gw, gb = pl.pallas_call(
@@ -487,10 +490,9 @@
             jax.ShapeDtypeStruct(gw.shape, F32),
             jax.ShapeDtypeStruct((1, share), F32),
         ),
-        in_specs=[anywhere] * 3 + [vmem],
+        in_specs=[vmem] * 4,
         out_specs=(anywhere,) * 3 + (vmem,),
         scratch_shapes=[dma((3, kk))],
-        compiler_params=pltpu.CompilerParams(vmem_limit_bytes=56 * 1024 * 1024),
     )(out, gf, gw, gb)
     return (out.reshape(fields.shape), gf.reshape(fields.shape), gw, gb.reshape(share))
 

time: 91.1 us -> 49.1 us (0.54)
  Pallas kernels: 87.5 us -> 48.3 us
  local copies, waits for them, and re-layouts: 2.65 us -> 0 us
    pallas_call x1, Pallas kernels: 42.1 us -> 2.92 us  [on_device(): pl.pallas_call(functools.partial(hand_on, n), out_shape=(jax.ShapeDtypeSt...]
    unnamed x1 -> x0, local copies, waits for them, and re-layouts: 1.34 us -> none
    reshape x1 -> x0, local copies, waits for them, and re-layouts: 1.31 us -> none  [on_device(): taps = psi_near.transpose(2, 3, 1, 0).reshape(9 * kk, psi_near.shape[0])]
where the time goes in v3:
time: 49.1 us; the launch traced here: 48.9 us
  Pallas kernels  48.3 us (98%)
  between operations  0.64 us (1%)
    pallas_call x1, Pallas kernels, on_device(): pl.pallas_call(functools.partial(kernel, n, nrow, nl, kk, scale), out_sha...  45.4 us
    pallas_call x1, Pallas kernels, on_device(): pl.pallas_call(functools.partial(hand_on, n), out_shape=(jax.ShapeDtypeSt...  2.92 us

profile of v3, /device:TPU:0, one launch (start us, length us, event | category | flops | bytes accessed | tf_op | source)
XLA Modules:
  0.0 48.9 jit_solution(10756754732596232982)
XLA Ops:
  0.6 45.4 %shard_map.102 = (bf16[512,512]{1,0:T(8,128)(2,1)}, bf16[512,512]{1,0:T(8,128)(2,1)}, f32[4,32,512]{2,1,0:T(8,128)}, f32[8,512]{1,0:T(8,128)}) custom-call(bf16[512,512]{1,0:T(8,128)(2,1)} %bitcast.11, bf16[512,512]{1,0:T(8,128)(2,1)} %bitcast.12, bf16[3,3,4,128]{3,2,1,0:T(4,128)(2,1)} %bitcast.16, bf16[96,16]{1,0:T(8,128)(2,1)} %bitcast.15, ...), custom_call_target="tpu_custom_call" | custom-call | flops 4294967296 | bytes 8388608 | tf_op jit(solution)/shard_map/pallas_call | solution.py:429
  46.0 2.9 %shard_map.103 = (bf16[512,512]{1,0:T(8,128)(2,1)}, bf16[512,512]{1,0:T(8,128)(2,1)}, f32[4,32,512]{2,1,0:T(8,128)}, f32[1,32]{1,0:T(1,128)}) custom-call(bf16[512,512]{1,0:T(8,128)(2,1)} %get-tuple-element.12.out_in, bf16[512,512]{1,0:T(8,128)(2,1)} %get-tuple-element.13.gf_in, f32[4,32,512]{2,1,0:T(8,128)} %get-tuple-element.14.gw_in, ...), custom_call_target="tpu_custom_call" | custom-call | tf_op jit(solution)/shard_map/pallas_call | solution.py:485

commit v4 on v3

--- a/solution.py
+++ b/solution.py
@@ -62,9 +62,7 @@
         return 0
 
     lax.fori_loop(1, 2 * n, greet, 0)
-    bsend[...] = jnp.broadcast_to(
-        jnp.sum(g_ref[...].astype(F32), axis=0, keepdims=True), bsend.shape
-    )
+    bsend[...] = jnp.sum(g_ref[...].astype(F32), axis=0, keepdims=True)
     rid = lax.broadcasted_iota(jnp.int32, (2 * nrow, nrow * nl), 0)
     cid = lax.broadcasted_iota(jnp.int32, (2 * nrow, nrow * nl), 1)
     want = lax.rem(rid, nrow) * nl + jnp.where(rid < nrow, 0, nl - 1)
@@ -354,10 +352,6 @@
             s2[k, q] = own[k, q, par].astype(BF16)
         loop(1, nz, lambda step: copy2(k, step).start())
 
-    loop(0, kk, stage2)
-
-    inner(1)
-    edges(1)
 
     def backward(b):
         at = pl.ds(pl.multiple_of(b * step_rows, step_rows), step_rows)
@@ -369,11 +363,17 @@
             acc = term if acc is None else acc + term
         gf_ref[at, :] = acc.astype(BF16)
 
+    stage2(0)
+    inner(1)
+    stage2(1)
+    edges(1)
+    loop(2, kk - 1, stage2)
     loop(0, nrow * nl // step_rows, backward)
     store_gf.start()
+    stage2(kk - 1)
 
     loop(1, 2 * n, lambda step: bias_copy(step).wait())
-    gb_ref[...] = jnp.sum(brecv[...], axis=0) * scale
+    gb_ref[...] = jnp.broadcast_to(jnp.sum(brecv[...], axis=0) * scale, gb_ref.shape)
 
     def final(k):
         gw_ref[k] = own[k, zz, par]
@@ -461,8 +461,8 @@
             pltpu.VMEM((kk, nz, cr, chan), BF16),
             pltpu.VMEM((kk, nz, cr, chan), BF16),
             pltpu.VMEM((kk, nz, cr, chan), BF16),
-            pltpu.VMEM((8, chan), F32),
-            pltpu.VMEM((2 * n, 8, chan), F32),
+            pltpu.VMEM((1, chan), F32),
+            pltpu.VMEM((2 * n, 1, chan), F32),
             dma((2, 5)), dma((2, 5)),
             dma((2, n)), dma((2, n)),
             dma((kk,)), dma((kk,)),

time: 49.1 us -> 46.2 us (0.941)
  Pallas kernels: 48.3 us -> 45.4 us
    pallas_call x1, Pallas kernels: 45.4 us -> 42.5 us  [on_device(): pl.pallas_call(functools.partial(kernel, n, nrow, nl, kk, scale), out_sha...]
where the time goes in v4:
time: 46.2 us; the launch traced here: 46 us
  Pallas kernels  45.4 us (98%)
  between operations  0.64 us (1%)
    pallas_call x1, Pallas kernels, on_device(): pl.pallas_call(functools.partial(kernel, n, nrow, nl, kk, scale), out_sha...  42.5 us
    pallas_call x1, Pallas kernels, on_device(): pl.pallas_call(functools.partial(hand_on, n), out_shape=(jax.ShapeDtypeSt...  2.92 us

profile of v4, /device:TPU:0, one launch (start us, length us, event | category | flops | bytes accessed | tf_op | source)
XLA Modules:
  0.0 46.0 jit_solution(15971952478639528300)
XLA Ops:
  0.6 42.5 %shard_map.102 = (bf16[512,512]{1,0:T(8,128)(2,1)}, bf16[512,512]{1,0:T(8,128)(2,1)}, f32[4,32,512]{2,1,0:T(8,128)}, f32[8,512]{1,0:T(8,128)}) custom-call(bf16[512,512]{1,0:T(8,128)(2,1)} %bitcast.11, bf16[512,512]{1,0:T(8,128)(2,1)} %bitcast.12, bf16[3,3,4,128]{3,2,1,0:T(4,128)(2,1)} %bitcast.16, bf16[96,16]{1,0:T(8,128)(2,1)} %bitcast.15, ...), custom_call_target="tpu_custom_call" | custom-call | flops 4294967296 | bytes 8388608 | tf_op jit(solution)/shard_map/pallas_call | solution.py:429
  43.1 2.9 %shard_map.103 = (bf16[512,512]{1,0:T(8,128)(2,1)}, bf16[512,512]{1,0:T(8,128)(2,1)}, f32[4,32,512]{2,1,0:T(8,128)}, f32[1,32]{1,0:T(1,128)}) custom-call(bf16[512,512]{1,0:T(8,128)(2,1)} %get-tuple-element.12.out_in, bf16[512,512]{1,0:T(8,128)(2,1)} %get-tuple-element.13.gf_in, f32[4,32,512]{2,1,0:T(8,128)} %get-tuple-element.14.gw_in, ...), custom_call_target="tpu_custom_call" | custom-call | tf_op jit(solution)/shard_map/pallas_call | solution.py:485
